TPU v7x, 32 devices: a whole 2x2x4 slice. The times are simulated.
32 devices in a mesh: groups: 2 (over x), ctx: 16 (over z, y, core).
Axes of the slice: x: 2, y: 2, z: 4, core: 2. Of those that a mesh axis runs over, the one named last changes fastest.
Arguments:
- queries: bfloat16 [4096, 2048], P(('groups', 'ctx')), parts along dimension 0, may hold values from -22 to 22
- key_rows: bfloat16 [4096, 512], P(('groups', 'ctx')), parts along dimension 0, may hold values from -4 to 4
- value_rows: bfloat16 [4096, 512], P(('groups', 'ctx')), parts along dimension 0, may hold values from -6 to 6
- output_gradient: bfloat16 [4096, 2048], P(('groups', 'ctx')), parts along dimension 0, may hold values from -6 to 6
- lengths: int32 [16], P('groups'), parts along dimension 0, may hold values from 1 to 512, 2048 in all
Outputs:
- attended: bfloat16 [4096, 2048], P(('groups', 'ctx')), parts along dimension 0
- grad_queries: bfloat16 [4096, 2048], P(('groups', 'ctx')), parts along dimension 0
- key_gradient: bfloat16 [4096, 512], P(('groups', 'ctx')), parts along dimension 0
- value_gradient: bfloat16 [4096, 512], P(('groups', 'ctx')), parts along dimension 0
There are 2 independent parts, one for each index of `groups`. A program takes and returns all parts, laid end to end along the dimension named above; each array names one. Nothing has to cross between parts.
Inputs may be any that keep to these rules, and one draw needn't show every extreme that they name: `lengths`: each document has 1 to 512 tokens, one exactly 512; they sum to 2048.
All inputs are finite; a program needn't handle non-finite values.
Results may differ from a plain program's by a relative error of at most 0.035.
Values may be sent and summed in bfloat16 or wider, within the bound.
A program may use at most 128 MiB of HBM per device.

v0:
```python
import functools
import math

import jax
import jax.numpy as jnp
from jax import lax
from jax.experimental import pallas as pl
from jax.experimental.pallas import tpu as pltpu
from jax.sharding import PartitionSpec as P

KV_HEADS = 4
HEAD = 128
GROUP = 4
HALF_HEADS = KV_HEADS // 2
PAIR = 128
BLOCK = 64
WINDOW = 5 * PAIR
WIDE = GROUP * HEAD
NEGATIVE_FLOOR = -1e30
SCALE = 1.0 / math.sqrt(HEAD)


def kernel(
    chips,
    lengths_ref,
    q_hbm,
    k_hbm,
    v_hbm,
    g_hbm,
    out_hbm,
    dq_hbm,
    dk_hbm,
    dv_hbm,
    qbuf,
    gbuf,
    kvbuf,
    obuf,
    dqbuf,
    kept,
    up_send,
    up_recv,
    sum_send,
    sum_recv,
    final,
    local_sem,
    swap_send,
    swap_recv,
    kv_send,
    kv_recv,
    grad_send,
    grad_recv,
    out_local,
    out_send,
    out_recv,
    fin_local,
    fin_send,
    fin_recv,
):
    ctx = lax.axis_index("ctx")
    chip = ctx // 2
    core = ctx - 2 * chip
    other = 1 - core
    sibling = 2 * chip + other
    last = 2 * chips - 1

    def place(side):
        return chip + side * (last - 2 * chip)

    def half_of(side, core_id):
        return core_id + side * (1 - 2 * core_id)

    def owner(t):
        return jnp.where(t < chips, t, last - t)

    def side_of(t):
        return jnp.where(t < chips, 0, 1)

    def remote(src, dst, send, recv, device):
        return pltpu.make_async_remote_copy(
            src_ref=src,
            dst_ref=dst,
            send_sem=send,
            recv_sem=recv,
            device_id={"ctx": device},
            device_id_type=pl.DeviceIdType.MESH,
        )

    @pl.when(chip < 2)
    def _():
        for h in range(HALF_HEADS):
            kvbuf[0, h, 0 : 4 * PAIR, :] = jnp.zeros((4 * PAIR, 2 * HEAD), jnp.bfloat16)

    barrier = pltpu.get_barrier_semaphore()
    pl.semaphore_signal(
        barrier, inc=1, device_id={"ctx": sibling}, device_id_type=pl.DeviceIdType.MESH
    )
    for step in (-2, -1, 1, 2):
        peer = chip + step

        @pl.when((peer >= 0) & (peer < chips))
        def _():
            pl.semaphore_signal(
                barrier,
                inc=1,
                device_id={"ctx": 2 * peer + core},
                device_id_type=pl.DeviceIdType.MESH,
            )

    count = 1
    for step in (-2, -1, 1, 2):
        peer = chip + step
        count = count + jnp.where((peer >= 0) & (peer < chips), 1, 0)
    pl.semaphore_wait(barrier, count)

    def kv_stage(s, h, x, who):
        src = (k_hbm, v_hbm)[x].at[
            pl.ds(s * BLOCK, BLOCK), pl.ds(pl.multiple_of((who * HALF_HEADS + h) * HEAD, HEAD), HEAD)
        ]
        rows = pl.multiple_of(4 * PAIR + half_of(s, core) * BLOCK, BLOCK)
        dst = kvbuf.at[s, h, pl.ds(rows, BLOCK), pl.ds(x * HEAD, HEAD)]
        return src, dst

    def q_stage(s, h, x, who):
        src = (q_hbm, g_hbm)[x].at[
            pl.ds(s * BLOCK, BLOCK), pl.ds(pl.multiple_of((who * HALF_HEADS + h) * WIDE, WIDE), WIDE)
        ]
        rows = pl.multiple_of(half_of(s, core) * BLOCK, BLOCK)
        dst = (qbuf, gbuf)[x].at[s, h, pl.ds(rows, BLOCK), :]
        return src, dst

    def staged(kind, s, h, x):
        stage = (kv_stage, q_stage)[kind]
        src, dst = stage(s, h, x, core)
        mine = pltpu.make_async_copy(src, dst, local_sem.at[kind, s, h, x])
        src, dst = stage(s, h, x, other)
        swap = remote(
            src, dst, swap_send.at[kind, s, h, x], swap_recv.at[kind, s, h, x], sibling
        )
        return mine, swap

    order = [(s, h, x) for h in range(HALF_HEADS) for s in range(2) for x in range(2)]
    for kind in range(2):
        for s, h, x in order:
            mine, swap = staged(kind, s, h, x)
            swap.start()
            mine.start()

    def forward(s, h, step):
        t = place(s) + step
        rows = (4 - step) * PAIR
        src = kvbuf.at[s, h, pl.ds(4 * PAIR, PAIR), :]
        dst = kvbuf.at[side_of(t), h, pl.ds(rows, PAIR), :]
        return t, remote(
            src,
            dst,
            kv_send.at[s, h, step - 1],
            kv_recv.at[side_of(t), h, step - 1],
            2 * owner(t) + core,
        )

    def forward_self(h):
        return pltpu.make_async_copy(
            kvbuf.at[0, h, pl.ds(4 * PAIR, PAIR), :],
            kvbuf.at[1, h, pl.ds(3 * PAIR, PAIR), :],
            kv_recv.at[1, h, 0],
        )

    def relay(s, h):
        t = place(s) + 2
        return t, remote(
            kvbuf.at[s, h, pl.ds(2 * PAIR, 2 * PAIR), :],
            kvbuf.at[side_of(t), h, pl.ds(0, 2 * PAIR), :],
            kv_send.at[s, h, 2],
            kv_recv.at[side_of(t), h, 2],
            2 * owner(t) + core,
        )

    def arrived(s, h, kind):
        rows = ((3, 1), (2, 1), (0, 2))[kind]
        ref = kvbuf.at[s, h, pl.ds(rows[0] * PAIR, rows[1] * PAIR), :]
        return remote(ref, ref, kv_send.at[s, h, kind], kv_recv.at[s, h, kind], sibling)

    for h in range(HALF_HEADS):
        for s in range(2):
            for x in range(2):
                mine, swap = staged(0, s, h, x)
                mine.wait()
                swap.wait_recv()
            t, copy = forward(s, h, 2)
            pl.when(t <= last)(copy.start)
            t, copy = forward(s, h, 1)
            if s == 0:
                pl.when(chip < chips - 1)(copy.start)
                pl.when(chip == chips - 1)(forward_self(h).start)
            else:
                pl.when(t <= last)(copy.start)

    for h in range(HALF_HEADS):
        for s in range(2):
            here = place(s)
            pl.when(here >= 1)(arrived(s, h, 0).wait_recv)
            pl.when(here >= 2)(arrived(s, h, 1).wait_recv)
            t, copy = relay(s, h)
            pl.when(t <= last)(copy.start)

    def out_copies(s, h, x):
        buf = (obuf, dqbuf)[x]
        hbm = (out_hbm, dq_hbm)[x]
        columns = pl.ds(pl.multiple_of((core * HALF_HEADS + h) * WIDE, WIDE), WIDE)
        rows = pl.ds(pl.multiple_of(s * BLOCK, BLOCK), BLOCK)
        own = pl.ds(pl.multiple_of(half_of(s, core) * BLOCK, BLOCK), BLOCK)
        theirs = pl.ds(pl.multiple_of(half_of(s, other) * BLOCK, BLOCK), BLOCK)
        mine = pltpu.make_async_copy(
            buf.at[s, h, own, :], hbm.at[rows, columns], out_local.at[s, h, x]
        )
        swap = remote(
            buf.at[s, h, theirs, :],
            hbm.at[rows, columns],
            out_send.at[s, h, x],
            out_recv.at[s, h, x],
            sibling,
        )
        return mine, swap

    def partial_up(s, h):
        t = place(s) - 2
        return t, remote(
            up_send.at[s, h],
            up_recv.at[side_of(t), h],
            grad_send.at[s, h, 2],
            grad_recv.at[side_of(t), h, 2],
            2 * owner(t) + core,
        )

    def summed(s, h, step):
        t = place(s) - step
        rows = pl.ds((2 - step) * PAIR, PAIR)
        return t, remote(
            sum_send.at[s, h, rows, :],
            sum_recv.at[side_of(t), h, step - 1],
            grad_send.at[s, h, step - 1],
            grad_recv.at[side_of(t), h, step - 1],
            2 * owner(t) + core,
        )

    def summed_self(h):
        return pltpu.make_async_copy(
            sum_send.at[1, h, pl.ds(PAIR, PAIR), :],
            sum_recv.at[0, h, 0],
            grad_recv.at[0, h, 0],
        )

    def grad_arrived(s, h, kind):
        ref = up_recv.at[s, h] if kind == 2 else sum_recv.at[s, h, kind]
        return remote(ref, ref, grad_send.at[s, h, kind], grad_recv.at[s, h, kind], sibling)

    def compute(s, h):
        here = place(s)
        for x in range(2):
            mine, swap = staged(1, s, h, x)
            mine.wait()
            swap.wait_recv()
        pl.when(here >= 2)(arrived(s, h, 2).wait_recv)

        query_at = here * PAIR + lax.broadcasted_iota(jnp.int32, (1, PAIR), 1)
        start = jnp.zeros((1, PAIR), jnp.int32)
        end = jnp.int32(0)
        for doc in range(lengths_ref.shape[0]):
            end = end + lengths_ref[doc]
            start = jnp.maximum(start, jnp.where(end <= query_at, end, 0))
        key_at = (here - 4) * PAIR + lax.broadcasted_iota(jnp.int32, (WINDOW, PAIR), 0)
        visible = (key_at >= start) & (key_at <= query_at)
        bias = jnp.where(visible, 0.0, NEGATIVE_FLOOR).astype(jnp.float32)
        bias = jnp.concatenate([bias] * GROUP, axis=1)

        keys = kvbuf[s, h, :, 0:HEAD]
        values = kvbuf[s, h, :, HEAD : 2 * HEAD]
        q = jnp.concatenate(
            [qbuf[s, h, :, g * HEAD : (g + 1) * HEAD] for g in range(GROUP)], axis=0
        )
        grad = jnp.concatenate(
            [gbuf[s, h, :, g * HEAD : (g + 1) * HEAD] for g in range(GROUP)], axis=0
        )
        grad_t = grad.T
        scores = lax.dot_general(
            keys, q, (((1,), (1,)), ((), ())), preferred_element_type=jnp.float32
        )
        scores = scores + bias
        top = jnp.max(scores, axis=0, keepdims=True)
        weights = jnp.exp2((scores - top) * (SCALE * math.log2(math.e)))
        total = jnp.sum(weights, axis=0, keepdims=True)
        probs = weights * (1.0 / total)
        probs_b = probs.astype(jnp.bfloat16)
        attended_t = jnp.dot(values.T, probs_b, preferred_element_type=jnp.float32)
        attended_b = attended_t.astype(jnp.bfloat16)
        delta = jnp.sum(
            attended_b.astype(jnp.float32) * grad_t.astype(jnp.float32), axis=0, keepdims=True
        )
        dprob = jnp.dot(values, grad_t, preferred_element_type=jnp.float32)
        dscore = (probs * (dprob - delta)).astype(jnp.bfloat16)
        dq_t = jnp.dot(keys.T, dscore, preferred_element_type=jnp.float32) * SCALE
        dk = jnp.dot(dscore, q, preferred_element_type=jnp.float32) * SCALE
        dv = jnp.dot(probs_b, grad, preferred_element_type=jnp.float32)
        attended = attended_b.T
        dq = dq_t.astype(jnp.bfloat16).T
        for g in range(GROUP):
            obuf[s, h, :, g * HEAD : (g + 1) * HEAD] = attended[g * PAIR : (g + 1) * PAIR]
            dqbuf[s, h, :, g * HEAD : (g + 1) * HEAD] = dq[g * PAIR : (g + 1) * PAIR]
        up_send[s, h, :, 0:HEAD] = dk[0 : 2 * PAIR].astype(jnp.bfloat16)
        up_send[s, h, :, HEAD : 2 * HEAD] = dv[0 : 2 * PAIR].astype(jnp.bfloat16)
        t, copy = partial_up(s, h)
        pl.when(t >= 0)(copy.start)
        kept[s, h, :, 0:HEAD] = dk[2 * PAIR :]
        kept[s, h, :, HEAD : 2 * HEAD] = dv[2 * PAIR :]
        for x in range(2):
            mine, swap = out_copies(s, h, x)
            swap.start()
            mine.start()

    def pass_down(s, h):
        here = place(s)
        more = here + 2 <= last

        @pl.when(more)
        def _():
            grad_arrived(s, h, 2).wait_recv()
            sum_send[s, h] = (
                kept[s, h, 0 : 2 * PAIR, :] + up_recv[s, h].astype(jnp.float32)
            ).astype(jnp.bfloat16)

        @pl.when(jnp.logical_not(more))
        def _():
            sum_send[s, h] = kept[s, h, 0 : 2 * PAIR, :].astype(jnp.bfloat16)

        t, copy = summed(s, h, 2)
        pl.when(t >= 0)(copy.start)
        t, copy = summed(s, h, 1)
        at_self = here == chips
        pl.when((t >= 0) & jnp.logical_not(at_self))(copy.start)
        pl.when(at_self)(summed_self(h).start)

    def fin_copies(s, h, x):
        hbm = (dk_hbm, dv_hbm)[x]
        columns = pl.ds(pl.multiple_of((core * HALF_HEADS + h) * HEAD, HEAD), HEAD)
        rows = pl.ds(pl.multiple_of(s * BLOCK, BLOCK), BLOCK)
        own = pl.ds(pl.multiple_of(half_of(s, core) * BLOCK, BLOCK), BLOCK)
        theirs = pl.ds(pl.multiple_of(half_of(s, other) * BLOCK, BLOCK), BLOCK)
        cut = pl.ds(x * HEAD, HEAD)
        mine = pltpu.make_async_copy(
            final.at[s, h, own, cut], hbm.at[rows, columns], fin_local.at[s, h, x]
        )
        swap = remote(
            final.at[s, h, theirs, cut],
            hbm.at[rows, columns],
            fin_send.at[s, h, x],
            fin_recv.at[s, h, x],
            sibling,
        )
        return mine, swap

    def finish(s, h):
        here = place(s)
        for step in (1, 2):

            @pl.when(here + step <= last)
            def _():
                grad_arrived(s, h, step - 1).wait_recv()
                kept[s, h, 2 * PAIR :, :] += sum_recv[s, h, step - 1].astype(jnp.float32)

        final[s, h] = kept[s, h, 2 * PAIR :, :].astype(jnp.bfloat16)
        for x in range(2):
            mine, swap = fin_copies(s, h, x)
            swap.start()
            mine.start()

    def turn(i, carry):
        compute(lax.rem(i, 2), i // 2)

        @pl.when(i >= 2)
        def _():
            pass_down(lax.rem(i, 2), i // 2 - 1)

        return carry

    lax.fori_loop(0, 4, turn, 0)
    for s in range(2):
        pass_down(s, 1)
    for h in range(HALF_HEADS):
        for s in range(2):
            finish(s, h)

    for h in range(HALF_HEADS):
        for s in range(2):
            here = place(s)
            for x in range(2):
                for kind in range(2):
                    mine, swap = staged(kind, s, h, x)
                    swap.wait_send()
                for copies in (out_copies, fin_copies):
                    mine, swap = copies(s, h, x)
                    mine.wait()
                    swap.wait_send()
                    swap.wait_recv()
            t, copy = forward(s, h, 2)
            pl.when(t <= last)(copy.wait_send)
            t, copy = forward(s, h, 1)
            pl.when((t <= last) & (here != chips - 1))(copy.wait_send)
            t, copy = relay(s, h)
            pl.when(t <= last)(copy.wait_send)
            t, copy = partial_up(s, h)
            pl.when(t >= 0)(copy.wait_send)
            t, copy = summed(s, h, 2)
            pl.when(t >= 0)(copy.wait_send)
            t, copy = summed(s, h, 1)
            pl.when((t >= 0) & (here != chips))(copy.wait_send)


def on_device(queries, key_rows, value_rows, output_gradient, lengths):
    chips = lax.axis_size("ctx") // 2
    anywhere = pl.BlockSpec(memory_space=pl.ANY)
    bf16 = jnp.bfloat16
    dma = pltpu.SemaphoreType.DMA
    scratch = [
        pltpu.VMEM((2, 2, PAIR, WIDE), bf16),
        pltpu.VMEM((2, 2, PAIR, WIDE), bf16),
        pltpu.VMEM((2, 2, WINDOW, 2 * HEAD), bf16),
        pltpu.VMEM((2, 2, PAIR, WIDE), bf16),
        pltpu.VMEM((2, 2, PAIR, WIDE), bf16),
        pltpu.VMEM((2, 2, 3 * PAIR, 2 * HEAD), jnp.float32),
        pltpu.VMEM((2, 2, 2 * PAIR, 2 * HEAD), bf16),
        pltpu.VMEM((2, 2, 2 * PAIR, 2 * HEAD), bf16),
        pltpu.VMEM((2, 2, 2 * PAIR, 2 * HEAD), bf16),
        pltpu.VMEM((2, 2, 2, PAIR, 2 * HEAD), bf16),
        pltpu.VMEM((2, 2, PAIR, 2 * HEAD), bf16),
        dma((2, 2, 2, 2)),
        dma((2, 2, 2, 2)),
        dma((2, 2, 2, 2)),
        dma((2, 2, 3)),
        dma((2, 2, 3)),
        dma((2, 2, 3)),
        dma((2, 2, 3)),
    ] + [dma((2, 2, 2)) for _ in range(6)]
    return pl.pallas_call(
        functools.partial(kernel, chips),
        out_shape=tuple(
            jax.ShapeDtypeStruct(a.shape, bf16)
            for a in (queries, queries, key_rows, value_rows)
        ),
        in_specs=[pl.BlockSpec(memory_space=pltpu.SMEM)] + [anywhere] * 4,
        out_specs=(anywhere,) * 4,
        scratch_shapes=scratch,
        compiler_params=pltpu.CompilerParams(
            collective_id=0, has_side_effects=True, vmem_limit_bytes=40 * 1024 * 1024
        ),
    )(lengths, queries, key_rows, value_rows, output_gradient)


def solution(mesh):
    rows = P(("groups", "ctx"), None)
    return jax.shard_map(
        on_device,
        mesh=mesh,
        in_specs=(rows, rows, rows, rows, P("groups")),
        out_specs=(rows, rows, rows, rows),
        check_vma=False,
    )
```

profile of v0, /device:TPU:27, one launch (start us, length us, event | category | flops | bytes accessed | tf_op | source)
XLA Modules:
  0.0 45.9 jit_solution(8107004809284818180)
XLA Ops:
  0.6 0.0 copy-start
  0.6 1.0 %copy-done = bf16[128,2048]{1,0:T(8,128)(2,1)S(1)} copy-done((bf16[128,2048]{1,0:T(8,128)(2,1)S(1)}, bf16[128,2048]{1,0:T(8,128)(2,1)}, u32[]{:S(2)}) %copy-start) | copy-done | bytes 524312
  1.7 0.0 copy-start.1
  1.7 1.0 %copy-done.1 = bf16[128,2048]{1,0:T(8,128)(2,1)S(1)} copy-done((bf16[128,2048]{1,0:T(8,128)(2,1)S(1)}, bf16[128,2048]{1,0:T(8,128)(2,1)}, u32[]{:S(2)}) %copy-start.1) | copy-done | bytes 524312
  2.7 0.0 copy-start.2
  2.7 0.9 %copy-done.2 = bf16[128,512]{1,0:T(8,128)(2,1)S(1)} copy-done((bf16[128,512]{1,0:T(8,128)(2,1)S(1)}, bf16[128,512]{1,0:T(8,128)(2,1)}, u32[]{:S(2)}) %copy-start.2) | copy-done | bytes 131096
  3.6 0.0 copy-start.3
  3.6 0.9 %copy-done.3 = bf16[128,512]{1,0:T(8,128)(2,1)S(1)} copy-done((bf16[128,512]{1,0:T(8,128)(2,1)S(1)}, bf16[128,512]{1,0:T(8,128)(2,1)}, u32[]{:S(2)}) %copy-start.3) | copy-done | bytes 131096
  4.5 0.0 copy-start.4
  4.5 0.7 %copy-done.4 = s32[8]{0:T(128)S(1)} copy-done((s32[8]{0:T(128)S(1)}, s32[8]{0:T(128)}, u32[]{:S(2)}) %copy-start.4) | copy-done | bytes 56
  5.2 37.8 %shard_map.84 = (bf16[128,2048]{1,0:T(8,128)(2,1)S(1)}, bf16[128,2048]{1,0:T(8,128)(2,1)S(1)}, bf16[128,512]{1,0:T(8,128)(2,1)S(1)}, bf16[128,512]{1,0:T(8,128)(2,1)S(1)}) custom-call(s32[8]{0:T(128)S(1)} %copy-done.4, bf16[128,2048]{1,0:T(8,128)(2,1)S(1)} %copy-done, bf16[128,512]{1,0:T(8,128)(2,1)S(1)} %copy-done.2, bf16[128,512]{1,0:T(8,128)(2,1)S(1)} %copy-done.3, ...), custom_call_target="tpu_custom_call" | custom-call | tf_op jit(solution)/shard_map/pallas_call | solution.py:443
  43.0 0.8 %copy.13 = bf16[128,2048]{1,0:T(8,128)(2,1)} copy(bf16[128,2048]{1,0:T(8,128)(2,1)S(1)} %get-tuple-element.8) | data formatting | bytes 1048576
  43.8 0.8 %copy.14 = bf16[128,2048]{1,0:T(8,128)(2,1)} copy(bf16[128,2048]{1,0:T(8,128)(2,1)S(1)} %get-tuple-element.9) | data formatting | bytes 1048576
  44.6 0.7 %copy.15 = bf16[128,512]{1,0:T(8,128)(2,1)} copy(bf16[128,512]{1,0:T(8,128)(2,1)S(1)} %get-tuple-element.10) | data formatting | bytes 262144
  45.3 0.7 %copy.16 = bf16[128,512]{1,0:T(8,128)(2,1)} copy(bf16[128,512]{1,0:T(8,128)(2,1)S(1)} %get-tuple-element.11) | data formatting | bytes 262144
Async XLA Ops:
  0.6 1.0 %copy-start = (bf16[128,2048]{1,0:T(8,128)(2,1)S(1)}, bf16[128,2048]{1,0:T(8,128)(2,1)}, u32[]{:S(2)}) copy-start(bf16[128,2048]{1,0:T(8,128)(2,1)} %q_hbm.1) | copy-start | bytes 1572868
  1.7 1.0 %copy-start.1 = (bf16[128,2048]{1,0:T(8,128)(2,1)S(1)}, bf16[128,2048]{1,0:T(8,128)(2,1)}, u32[]{:S(2)}) copy-start(bf16[128,2048]{1,0:T(8,128)(2,1)} %g_hbm.1) | copy-start | bytes 1572868
  2.7 0.9 %copy-start.2 = (bf16[128,512]{1,0:T(8,128)(2,1)S(1)}, bf16[128,512]{1,0:T(8,128)(2,1)}, u32[]{:S(2)}) copy-start(bf16[128,512]{1,0:T(8,128)(2,1)} %k_hbm.1) | copy-start | bytes 393220
  3.6 0.9 %copy-start.3 = (bf16[128,512]{1,0:T(8,128)(2,1)S(1)}, bf16[128,512]{1,0:T(8,128)(2,1)}, u32[]{:S(2)}) copy-start(bf16[128,512]{1,0:T(8,128)(2,1)} %v_hbm.1) | copy-start | bytes 393220
  4.5 0.7 %copy-start.4 = (s32[8]{0:T(128)S(1)}, s32[8]{0:T(128)}, u32[]{:S(2)}) copy-start(s32[8]{0:T(128)} %lengths_ref.1) | copy-start | bytes 100
where the time goes:
time: 46.2 us; the launch traced here: 45.9 us
  Pallas kernels  37.8 us (82%)
  local copies, waits for them, and re-layouts  7.44 us (16%)
  between operations  0.65 us (1%)
    pallas_call x1, Pallas kernels, on_device(): pl.pallas_call(functools.partial(kernel, chips), out_shape=tuple((jax.Sha...  37.8 us
    unnamed x14, local copies, waits for them, and re-layouts  7.44 us

commit v1 on v0

v1 whole, which is shorter than its diff:
```python
import functools
import math

import jax
import jax.numpy as jnp
from jax import lax
from jax.experimental import pallas as pl
from jax.experimental.pallas import tpu as pltpu
from jax.sharding import PartitionSpec as P

KV_HEADS = 4
HEAD = 128
GROUP = 4
HALF_HEADS = KV_HEADS // 2
PAIR = 128
BLOCK = 64
WINDOW = 5 * PAIR
WIDE = GROUP * HEAD
NEGATIVE_FLOOR = -1e30
SCALE = 1.0 / math.sqrt(HEAD)


def kernel(
    chips,
    lengths_ref,
    q_hbm,
    k_hbm,
    v_hbm,
    g_hbm,
    packed,
    qbuf,
    gbuf,
    kvbuf,
    obuf,
    dqbuf,
    kept,
    up_send,
    up_recv,
    sum_send,
    sum_recv,
    final,
    local_sem,
    swap_send,
    swap_recv,
    kv_send,
    kv_recv,
    grad_send,
    grad_recv,
    out_local,
    out_send,
    out_recv,
    fin_local,
    fin_send,
    fin_recv,
):
    ctx = lax.axis_index("ctx")
    chip = ctx // 2
    core = ctx - 2 * chip
    other = 1 - core
    sibling = 2 * chip + other
    last = 2 * chips - 1

    def place(side):
        return chip + side * (last - 2 * chip)

    def half_of(side, core_id):
        return core_id + side * (1 - 2 * core_id)

    def owner(t):
        return jnp.where(t < chips, t, last - t)

    def side_of(t):
        return jnp.where(t < chips, 0, 1)

    def remote(src, dst, send, recv, device):
        return pltpu.make_async_remote_copy(
            src_ref=src,
            dst_ref=dst,
            send_sem=send,
            recv_sem=recv,
            device_id={"ctx": device},
            device_id_type=pl.DeviceIdType.MESH,
        )

    partner = 2 * (chip + 1 - 2 * lax.rem(chip, 2)) + core

    def odd(s):
        return lax.rem(place(s), 2) == 1

    for slot in range(4):

        @pl.when(chip + slot < 4)
        def _():
            for h in range(HALF_HEADS):
                kvbuf[0, h, slot * PAIR : (slot + 1) * PAIR, :] = jnp.zeros(
                    (PAIR, 2 * HEAD), jnp.bfloat16
                )

    barrier = pltpu.get_barrier_semaphore()
    for device in (sibling, partner):
        pl.semaphore_signal(
            barrier, inc=1, device_id={"ctx": device}, device_id_type=pl.DeviceIdType.MESH
        )
    count = 2
    for step in (-2, 2):
        peer = chip + step
        near = (peer >= 0) & (peer < chips)

        @pl.when(near)
        def _():
            pl.semaphore_signal(
                barrier,
                inc=1,
                device_id={"ctx": 2 * peer + core},
                device_id_type=pl.DeviceIdType.MESH,
            )

        count = count + jnp.where(near, 1, 0)
    pl.semaphore_wait(barrier, count)

    def kv_stage(s, h, x, who):
        src = (k_hbm, v_hbm)[x].at[
            pl.ds(s * BLOCK, BLOCK), pl.ds(pl.multiple_of((who * HALF_HEADS + h) * HEAD, HEAD), HEAD)
        ]
        rows = pl.multiple_of(4 * PAIR + half_of(s, core) * BLOCK, BLOCK)
        dst = kvbuf.at[s, h, pl.ds(rows, BLOCK), pl.ds(x * HEAD, HEAD)]
        return src, dst

    def q_stage(s, h, x, who):
        src = (q_hbm, g_hbm)[x].at[
            pl.ds(s * BLOCK, BLOCK), pl.ds(pl.multiple_of((who * HALF_HEADS + h) * WIDE, WIDE), WIDE)
        ]
        rows = pl.multiple_of(half_of(s, core) * BLOCK, BLOCK)
        dst = (qbuf, gbuf)[x].at[s, h, pl.ds(rows, BLOCK), :]
        return src, dst

    def staged_mine(kind, s, h, x):
        src, dst = (kv_stage, q_stage)[kind](s, h, x, core)
        return pltpu.make_async_copy(src, dst, local_sem.at[kind, s, h, x])

    def staged_swap(kind, s, h, x):
        src, dst = (kv_stage, q_stage)[kind](s, h, x, other)
        return remote(
            src, dst, swap_send.at[kind, s, h, x], swap_recv.at[kind, s, h, x], sibling
        )

    order = [(s, h, x) for h in range(HALF_HEADS) for s in range(2) for x in range(2)]
    for kind in range(2):
        for s, h, x in order:
            staged_swap(kind, s, h, x).start()
            staged_mine(kind, s, h, x).start()

    def rows_of(slot):
        return pl.ds(slot * PAIR, PAIR)

    def forward(s, h, kind):
        t = place(s) + 2
        source, target = ((4, 3), (4, 2), (2, 0), (3, 1))[kind]
        return remote(
            kvbuf.at[s, h, rows_of(source), :],
            kvbuf.at[side_of(t), h, rows_of(target), :],
            kv_send.at[s, h, kind],
            kv_recv.at[side_of(t), h, kind],
            2 * owner(t) + core,
        )

    def across(s, h, source):
        return remote(
            kvbuf.at[s, h, rows_of(source), :],
            kvbuf.at[s, h, rows_of(3), :],
            kv_send.at[s, h, 0],
            kv_recv.at[s, h, 0],
            partner,
        )

    def arrived(s, h, kind):
        ref = kvbuf.at[s, h, rows_of((3, 2, 0, 1)[kind]), :]
        return remote(ref, ref, kv_send.at[s, h, kind], kv_recv.at[s, h, kind], sibling)

    def sends_own(t):
        return (t + 2 <= last) & (t + 2 != chips)

    def sends_relay(t):
        return sends_own(t) & (t + 2 != chips + 1)

    def odd_across(t):
        return (lax.rem(t, 2) == 1) & (t >= 3) & (t != chips + 1)

    def even_across(t):
        return (lax.rem(t, 2) == 0) & (t >= 2) & (t != chips)

    for h in range(HALF_HEADS):
        for s in range(2):
            here = place(s)
            for x in range(2):
                staged_mine(0, s, h, x).wait()
                staged_swap(0, s, h, x).wait_recv()
            pl.when(sends_own(here))(forward(s, h, 1).start)
            pl.when(jnp.logical_not(odd(s)))(across(s, h, 4).start)

    for h in range(HALF_HEADS):
        for s in range(2):
            here = place(s)
            pl.when((here >= 2) & (here != chips))(arrived(s, h, 1).wait_recv)
            pl.when(odd_across(here))(across(s, h, 2).start)
            pl.when((here >= 2) & (here != chips) & sends_relay(here))(forward(s, h, 2).start)

    for h in range(HALF_HEADS):
        for s in range(2):
            here = place(s)
            pl.when(odd(s) | even_across(here))(arrived(s, h, 0).wait_recv)
            if s == 1:

                @pl.when(here == chips)
                def _():
                    kvbuf[1, h, 2 * PAIR : 4 * PAIR, :] = kvbuf[0, h, 3 * PAIR : 5 * PAIR, :]
                    forward(1, h, 2).start()

            pl.when((here >= 1) & sends_relay(here))(forward(s, h, 3).start)

    def out_place(s, h, x):
        columns = pl.ds(
            pl.multiple_of(x * KV_HEADS * WIDE + (core * HALF_HEADS + h) * WIDE, WIDE), WIDE
        )
        return packed.at[pl.ds(pl.multiple_of(s * BLOCK, BLOCK), BLOCK), columns]

    def fin_place(s, h, x):
        start = 2 * KV_HEADS * WIDE + x * KV_HEADS * HEAD
        columns = pl.ds(pl.multiple_of(start + (core * HALF_HEADS + h) * HEAD, HEAD), HEAD)
        return packed.at[pl.ds(pl.multiple_of(s * BLOCK, BLOCK), BLOCK), columns]

    def half_rows(s, who):
        return pl.ds(pl.multiple_of(half_of(s, who) * BLOCK, BLOCK), BLOCK)

    def out_mine(s, h, x):
        src = (obuf, dqbuf)[x].at[s, h, half_rows(s, core), :]
        return pltpu.make_async_copy(src, out_place(s, h, x), out_local.at[s, h, x])

    def out_swap(s, h, x):
        src = (obuf, dqbuf)[x].at[s, h, half_rows(s, other), :]
        return remote(
            src, out_place(s, h, x), out_send.at[s, h, x], out_recv.at[s, h, x], sibling
        )

    def fin_mine(s, h, x):
        src = final.at[s, h, half_rows(s, core), pl.ds(x * HEAD, HEAD)]
        return pltpu.make_async_copy(src, fin_place(s, h, x), fin_local.at[s, h, x])

    def fin_swap(s, h, x):
        src = final.at[s, h, half_rows(s, other), pl.ds(x * HEAD, HEAD)]
        return remote(
            src, fin_place(s, h, x), fin_send.at[s, h, x], fin_recv.at[s, h, x], sibling
        )

    def partial_up(s, h):
        t = place(s) - 2
        return remote(
            up_send.at[s, h],
            up_recv.at[side_of(t), h],
            grad_send.at[s, h, 2],
            grad_recv.at[side_of(t), h, 2],
            2 * owner(t) + core,
        )

    def summed_back(s, h):
        t = place(s) - 2
        return remote(
            sum_send.at[s, h, pl.ds(0, PAIR), :],
            sum_recv.at[side_of(t), h, 1],
            grad_send.at[s, h, 1],
            grad_recv.at[side_of(t), h, 1],
            2 * owner(t) + core,
        )

    def summed_across(s, h):
        return remote(
            sum_send.at[s, h, pl.ds(PAIR, PAIR), :],
            sum_recv.at[s, h, 0],
            grad_send.at[s, h, 0],
            grad_recv.at[s, h, 0],
            partner,
        )

    def grad_arrived(s, h, kind):
        ref = up_recv.at[s, h] if kind == 2 else sum_recv.at[s, h, kind]
        return remote(ref, ref, grad_send.at[s, h, kind], grad_recv.at[s, h, kind], sibling)

    def sends_up(t):
        return (t >= 2) & (t != chips) & (t != chips + 1)

    def sends_back(t):
        return (t >= 2) & (t != chips)

    def compute(s, h):
        here = place(s)
        for x in range(2):
            staged_mine(1, s, h, x).wait()
            staged_swap(1, s, h, x).wait_recv()
        relayed = (here != chips) & (here != chips + 1)
        relayed = relayed & jnp.logical_not((s == 0) & (chip == chips - 1))
        pl.when((here >= 4) & relayed)(arrived(s, h, 2).wait_recv)
        pl.when((here >= 3) & relayed)(arrived(s, h, 3).wait_recv)


        query_at = here * PAIR + lax.broadcasted_iota(jnp.int32, (1, PAIR), 1)
        start = jnp.zeros((1, PAIR), jnp.int32)
        end = jnp.int32(0)
        for doc in range(lengths_ref.shape[0]):
            end = end + lengths_ref[doc]
            start = jnp.maximum(start, jnp.where(end <= query_at, end, 0))
        key_at = (here - 4) * PAIR + lax.broadcasted_iota(jnp.int32, (WINDOW, PAIR), 0)
        visible = (key_at >= start) & (key_at <= query_at)
        bias = jnp.where(visible, 0.0, NEGATIVE_FLOOR).astype(jnp.float32)
        bias = jnp.concatenate([bias] * GROUP, axis=1)

        @pl.when(here == chips)
        def _():
            before = place(0)
            pl.when(before >= 4)(arrived(0, h, 2).wait_recv)
            pl.when(before >= 3)(arrived(0, h, 3).wait_recv)
            kvbuf[1, h, 0 : 2 * PAIR, :] = kvbuf[0, h, PAIR : 3 * PAIR, :]

        @pl.when(here == chips + 1)
        def _():
            kvbuf[1, h, 0 : 2 * PAIR, :] = kvbuf[0, h, 3 * PAIR : 5 * PAIR, :]

        keys = kvbuf[s, h, :, 0:HEAD]
        values = kvbuf[s, h, :, HEAD : 2 * HEAD]
        q = jnp.concatenate(
            [qbuf[s, h, :, g * HEAD : (g + 1) * HEAD] for g in range(GROUP)], axis=0
        )
        grad = jnp.concatenate(
            [gbuf[s, h, :, g * HEAD : (g + 1) * HEAD] for g in range(GROUP)], axis=0
        )
        grad_t = grad.T
        scores = lax.dot_general(
            keys, q, (((1,), (1,)), ((), ())), preferred_element_type=jnp.float32
        )
        scores = scores + bias
        top = jnp.max(scores, axis=0, keepdims=True)
        weights = jnp.exp2((scores - top) * (SCALE * math.log2(math.e)))
        total = jnp.sum(weights, axis=0, keepdims=True)
        probs = weights * (1.0 / total)
        probs_b = probs.astype(jnp.bfloat16)
        attended_t = jnp.dot(values.T, probs_b, preferred_element_type=jnp.float32)
        attended_b = attended_t.astype(jnp.bfloat16)
        delta = jnp.sum(
            attended_b.astype(jnp.float32) * grad_t.astype(jnp.float32), axis=0, keepdims=True
        )
        dprob = jnp.dot(values, grad_t, preferred_element_type=jnp.float32)
        dscore = (probs * (dprob - delta)).astype(jnp.bfloat16)
        dq_t = jnp.dot(keys.T, dscore, preferred_element_type=jnp.float32) * SCALE
        dk = jnp.dot(dscore, q, preferred_element_type=jnp.float32) * SCALE
        dv = jnp.dot(probs_b, grad, preferred_element_type=jnp.float32)
        attended = attended_b.T
        dq = dq_t.astype(jnp.bfloat16).T
        for g in range(GROUP):
            obuf[s, h, :, g * HEAD : (g + 1) * HEAD] = attended[g * PAIR : (g + 1) * PAIR]
            dqbuf[s, h, :, g * HEAD : (g + 1) * HEAD] = dq[g * PAIR : (g + 1) * PAIR]
        up_send[s, h, :, 0:HEAD] = dk[0 : 2 * PAIR].astype(jnp.bfloat16)
        up_send[s, h, :, HEAD : 2 * HEAD] = dv[0 : 2 * PAIR].astype(jnp.bfloat16)
        kept[s, h, :, 0:HEAD] = dk[2 * PAIR :]
        kept[s, h, :, HEAD : 2 * HEAD] = dv[2 * PAIR :]

        @pl.when((s == 0) & (chip == chips - 1))
        def _():
            up_send[0, h, PAIR:, :] += up_send[1, h, 0:PAIR, :]
            kept[0, h, 0:PAIR, :] += up_send[1, h, PAIR:, :].astype(jnp.float32)

        @pl.when((s == 0) & (chip == chips - 2))
        def _():
            kept[0, h, PAIR:, :] += up_send[1, h].astype(jnp.float32)

        pl.when(sends_up(here))(partial_up(s, h).start)
        for x in range(2):
            out_swap(s, h, x).start()
            out_mine(s, h, x).start()

    def pass_down(s, h):
        here = place(s)

        @pl.when(sends_relay(here))
        def _():
            grad_arrived(s, h, 2).wait_recv()
            kept[s, h, 0 : 2 * PAIR, :] += up_recv[s, h].astype(jnp.float32)

        @pl.when(here == chips)
        def _():
            kept[0, h, PAIR:, :] += kept[1, h, 0 : 2 * PAIR, :]

        sum_send[s, h, PAIR:, :] = kept[s, h, PAIR : 2 * PAIR, :].astype(jnp.bfloat16)
        pl.when(odd(s) | even_across(here))(summed_across(s, h).start)

        @pl.when(jnp.logical_not(odd(s)))
        def _():
            sum_send[s, h, 0:PAIR, :] = kept[s, h, 0:PAIR, :].astype(jnp.bfloat16)
            pl.when(sends_back(here))(summed_back(s, h).start)

    def pass_odd(s, h):
        here = place(s)

        @pl.when(odd(s))
        def _():
            @pl.when(odd_across(here))
            def _():
                grad_arrived(s, h, 0).wait_recv()
                kept[s, h, 0:PAIR, :] += sum_recv[s, h, 0].astype(jnp.float32)

            sum_send[s, h, 0:PAIR, :] = kept[s, h, 0:PAIR, :].astype(jnp.bfloat16)
            pl.when(sends_back(here))(summed_back(s, h).start)

    def finish(s, h):
        here = place(s)

        @pl.when(jnp.logical_not(odd(s)))
        def _():
            grad_arrived(s, h, 0).wait_recv()
            kept[s, h, 2 * PAIR :, :] += sum_recv[s, h, 0].astype(jnp.float32)

        @pl.when(sends_own(here))
        def _():
            grad_arrived(s, h, 1).wait_recv()
            kept[s, h, 2 * PAIR :, :] += sum_recv[s, h, 1].astype(jnp.float32)

        final[s, h] = kept[s, h, 2 * PAIR :, :].astype(jnp.bfloat16)
        for x in range(2):
            fin_swap(s, h, x).start()
            fin_mine(s, h, x).start()

    def turn(i, carry):
        side = 1 - lax.rem(i, 2)
        half = i // 2

        compute(side, half)

        @pl.when(i >= 2)
        def _():
            pass_down(side, half - 1)

        return carry

    lax.fori_loop(0, 4, turn, 0)
    for s in range(2):
        pass_odd(s, 0)
    for s in (1, 0):
        pass_down(s, 1)
    for s in range(2):
        pass_odd(s, 1)
    for h in range(HALF_HEADS):
        for s in range(2):
            finish(s, h)

    for h in range(HALF_HEADS):
        for s in range(2):
            here = place(s)
            for x in range(2):
                for kind in range(2):
                    staged_swap(kind, s, h, x).wait_send()
                out_mine(s, h, x).wait()
                fin_mine(s, h, x).wait()
                for swap in (out_swap, fin_swap):
                    swap(s, h, x).wait_send()
                    swap(s, h, x).wait_recv()
            pl.when(sends_own(here))(forward(s, h, 1).wait_send)
            pl.when(jnp.logical_not(odd(s)) | odd_across(here))(across(s, h, 4).wait_send)
            pl.when((here >= 2) & sends_relay(here))(forward(s, h, 2).wait_send)
            pl.when((here >= 1) & sends_relay(here))(forward(s, h, 3).wait_send)
            pl.when(sends_up(here))(partial_up(s, h).wait_send)
            pl.when(odd(s) | even_across(here))(summed_across(s, h).wait_send)
            pl.when(sends_back(here))(summed_back(s, h).wait_send)


def split_kernel(packed, out, dq, dk, dv, b0, b1, b2, b3, sem):
    ins, outs = [], []
    start = 0
    for i, (ref, buf) in enumerate(zip((out, dq, dk, dv), (b0, b1, b2, b3))):
        width = ref.shape[1]
        ins.append(pltpu.make_async_copy(packed.at[:, pl.ds(start, width)], buf, sem.at[0, i]))
        outs.append(pltpu.make_async_copy(buf, ref, sem.at[1, i]))
        start += width
    for copy in ins:
        copy.start()
    for a, b in zip(ins, outs):
        a.wait()
        b.start()
    for copy in outs:
        copy.wait()


def on_device(queries, key_rows, value_rows, output_gradient, lengths):
    chips = lax.axis_size("ctx") // 2
    anywhere = pl.BlockSpec(memory_space=pl.ANY)
    bf16 = jnp.bfloat16
    dma = pltpu.SemaphoreType.DMA
    scratch = [
        pltpu.VMEM((2, 2, PAIR, WIDE), bf16),
        pltpu.VMEM((2, 2, PAIR, WIDE), bf16),
        pltpu.VMEM((2, 2, WINDOW, 2 * HEAD), bf16),
        pltpu.VMEM((2, 2, PAIR, WIDE), bf16),
        pltpu.VMEM((2, 2, PAIR, WIDE), bf16),
        pltpu.VMEM((2, 2, 3 * PAIR, 2 * HEAD), jnp.float32),
        pltpu.VMEM((2, 2, 2 * PAIR, 2 * HEAD), bf16),
        pltpu.VMEM((2, 2, 2 * PAIR, 2 * HEAD), bf16),
        pltpu.VMEM((2, 2, 2 * PAIR, 2 * HEAD), bf16),
        pltpu.VMEM((2, 2, 2, PAIR, 2 * HEAD), bf16),
        pltpu.VMEM((2, 2, PAIR, 2 * HEAD), bf16),
        dma((2, 2, 2, 2)),
        dma((2, 2, 2, 2)),
        dma((2, 2, 2, 2)),
        dma((2, 2, 4)),
        dma((2, 2, 4)),
        dma((2, 2, 3)),
        dma((2, 2, 3)),
    ] + [dma((2, 2, 2)) for _ in range(6)]
    hbm = pl.BlockSpec(memory_space=pltpu.HBM)
    rows = queries.shape[0]
    outs = (queries, queries, key_rows, value_rows)
    packed = pl.pallas_call(
        functools.partial(kernel, chips),
        out_shape=jax.ShapeDtypeStruct((rows, sum(a.shape[1] for a in outs)), bf16),
        in_specs=[pl.BlockSpec(memory_space=pltpu.SMEM)] + [hbm] * 4,
        out_specs=anywhere,
        scratch_shapes=scratch,
        compiler_params=pltpu.CompilerParams(
            collective_id=0, has_side_effects=True, vmem_limit_bytes=61 * 1024 * 1024
        ),
    )(lengths, queries, key_rows, value_rows, output_gradient)
    return pl.pallas_call(
        split_kernel,
        out_shape=tuple(jax.ShapeDtypeStruct(a.shape, bf16) for a in outs),
        in_specs=[anywhere],
        out_specs=(hbm,) * 4,
        scratch_shapes=[pltpu.VMEM(a.shape, bf16) for a in outs] + [dma((2, 4))],
    )(packed)


def solution(mesh):
    rows = P(("groups", "ctx"), None)
    return jax.shard_map(
        on_device,
        mesh=mesh,
        in_specs=(rows, rows, rows, rows, P("groups")),
        out_specs=(rows, rows, rows, rows),
        check_vma=False,
    )
```

time: 46.2 us -> 40.7 us (0.88)
  the two profiles are of different devices: /device:TPU:27 before, /device:TPU:7 now
where the time goes in v1:
time: 40.7 us; the launch traced here: 40.5 us
  Pallas kernels  39.9 us (98%)
  between operations  0.64 us (2%)
    pallas_call x1, Pallas kernels, on_device(): pl.pallas_call(functools.partial(kernel, chips), out_shape=jax.ShapeDtype...  37.7 us
    pallas_call x1, Pallas kernels, on_device(): pl.pallas_call(split_kernel, out_shape=tuple((jax.ShapeDtypeStruct(a.shap...  2.16 us

profile of v1, /device:TPU:7, one launch (start us, length us, event | category | flops | bytes accessed | tf_op | source)
XLA Modules:
  0.0 40.5 jit_solution(5156436870615115791)
XLA Ops:
  0.6 37.7 %shard_map.84.packed = bf16[128,5120]{1,0:T(8,128)(2,1)} custom-call(s32[8]{0:T(128)} %lengths_ref.1, bf16[128,2048]{1,0:T(8,128)(2,1)} %q_hbm.1, bf16[128,512]{1,0:T(8,128)(2,1)} %k_hbm.1, bf16[128,512]{1,0:T(8,128)(2,1)} %v_hbm.1, bf16[128,2048]{1,0:T(8,128)(2,1)} %g_hbm.1), custom_call_target="tpu_custom_call" | custom-call | tf_op jit(solution)/shard_map/pallas_call | solution.py:518
  38.4 2.2 %shard_map.85 = (bf16[128,2048]{1,0:T(8,128)(2,1)}, bf16[128,2048]{1,0:T(8,128)(2,1)}, bf16[128,512]{1,0:T(8,128)(2,1)}, bf16[128,512]{1,0:T(8,128)(2,1)}) custom-call(bf16[128,5120]{1,0:T(8,128)(2,1)} %shard_map.84.packed), custom_call_target="tpu_custom_call" | custom-call | tf_op jit(solution)/shard_map/pallas_call | solution.py:528

commit v2 on v1

--- a/solution.py
+++ b/solution.py
@@ -46,6 +46,7 @@
     kv_recv,
     grad_send,
     grad_recv,
+    direct_send,
     out_local,
     out_send,
     out_recv,
@@ -97,25 +98,26 @@
                 )
 
     barrier = pltpu.get_barrier_semaphore()
-    for device in (sibling, partner):
+
+    def greet(device):
         pl.semaphore_signal(
             barrier, inc=1, device_id={"ctx": device}, device_id_type=pl.DeviceIdType.MESH
         )
-    count = 2
+
+    count = 3
+    greet(sibling)
+    for which in range(2):
+        greet(partner - core + which)
     for step in (-2, 2):
         peer = chip + step
         near = (peer >= 0) & (peer < chips)
 
         @pl.when(near)
         def _():
-            pl.semaphore_signal(
-                barrier,
-                inc=1,
-                device_id={"ctx": 2 * peer + core},
-                device_id_type=pl.DeviceIdType.MESH,
-            )
-
-        count = count + jnp.where(near, 1, 0)
+            for which in range(2):
+                greet(2 * peer + which)
+
+        count = count + jnp.where(near, 2, 0)
     pl.semaphore_wait(barrier, count)
 
     def kv_stage(s, h, x, who):
@@ -144,59 +146,81 @@
             src, dst, swap_send.at[kind, s, h, x], swap_recv.at[kind, s, h, x], sibling
         )
 
+    def rows_of(slot):
+        return pl.ds(slot * PAIR, PAIR)
+
+    def forward(s, h, kind):
+        t = place(s) + 2
+        source, target = ((4, 3), (4, 2), (2, 0), (3, 1))[kind]
+        return remote(
+            kvbuf.at[s, h, rows_of(source), :],
+            kvbuf.at[side_of(t), h, rows_of(target), :],
+            kv_send.at[s, h, kind],
+            kv_recv.at[side_of(t), h, kind],
+            2 * owner(t) + core,
+        )
+
+    def across(s, h, source):
+        return remote(
+            kvbuf.at[s, h, rows_of(source), :],
+            kvbuf.at[s, h, rows_of(3), :],
+            kv_send.at[s, h, 0],
+            kv_recv.at[s, h, 0],
+            partner,
+        )
+
+    def arrived(s, h, kind):
+        ref = kvbuf.at[s, h, rows_of((3, 2, 0, 1)[kind]), :]
+        return remote(ref, ref, kv_send.at[s, h, kind], kv_recv.at[s, h, kind], sibling)
+
+    def sends_own(t):
+        return (t + 2 <= last) & (t + 2 != chips)
+
+    def sends_relay(t):
+        return sends_own(t) & (t + 2 != chips + 1)
+
+    def odd_across(t):
+        return (lax.rem(t, 2) == 1) & (t >= 3) & (t != chips + 1)
+
+    def even_across(t):
+        return (lax.rem(t, 2) == 0) & (t >= 2) & (t != chips)
+
+    def direct(s, head, x, kind):
+        t = place(s) + 2 * kind
+        core_to = head // HALF_HEADS
+        h = head % HALF_HEADS
+        src = (k_hbm, v_hbm)[x].at[pl.ds(s * BLOCK, BLOCK), pl.ds(head * HEAD, HEAD)]
+        rows = pl.multiple_of((3 - kind) * PAIR + half_of(s, core) * BLOCK, BLOCK)
+        side = side_of(t) if kind else s
+        return remote(
+            src,
+            kvbuf.at[side, h, pl.ds(rows, BLOCK), pl.ds(x * HEAD, HEAD)],
+            direct_send.at[s, head, x, kind],
+            kv_recv.at[side, h, kind],
+            (2 * owner(t) if kind else partner - core) + core_to,
+        )
+
+    def each_direct(s, h, act):
+        def run(kind):
+            for head in (h, h + HALF_HEADS):
+                for x in range(2):
+                    act(direct(s, head, x, kind))
+
+        pl.when(sends_own(place(s)))(functools.partial(run, 1))
+        pl.when(jnp.logical_not(odd(s)))(functools.partial(run, 0))
+
+    for h in range(HALF_HEADS):
+        for s in range(2):
+            each_direct(s, h, lambda copy: copy.start())
     order = [(s, h, x) for h in range(HALF_HEADS) for s in range(2) for x in range(2)]
     for kind in range(2):
         for s, h, x in order:
             staged_swap(kind, s, h, x).start()
             staged_mine(kind, s, h, x).start()
 
-    def rows_of(slot):
-        return pl.ds(slot * PAIR, PAIR)
-
-    def forward(s, h, kind):
-        t = place(s) + 2
-        source, target = ((4, 3), (4, 2), (2, 0), (3, 1))[kind]
-        return remote(
-            kvbuf.at[s, h, rows_of(source), :],
-            kvbuf.at[side_of(t), h, rows_of(target), :],
-            kv_send.at[s, h, kind],
-            kv_recv.at[side_of(t), h, kind],
-            2 * owner(t) + core,
-        )
-
-    def across(s, h, source):
-        return remote(
-            kvbuf.at[s, h, rows_of(source), :],
-            kvbuf.at[s, h, rows_of(3), :],
-            kv_send.at[s, h, 0],
-            kv_recv.at[s, h, 0],
-            partner,
-        )
-
-    def arrived(s, h, kind):
-        ref = kvbuf.at[s, h, rows_of((3, 2, 0, 1)[kind]), :]
-        return remote(ref, ref, kv_send.at[s, h, kind], kv_recv.at[s, h, kind], sibling)
-
-    def sends_own(t):
-        return (t + 2 <= last) & (t + 2 != chips)
-
-    def sends_relay(t):
-        return sends_own(t) & (t + 2 != chips + 1)
-
-    def odd_across(t):
-        return (lax.rem(t, 2) == 1) & (t >= 3) & (t != chips + 1)
-
-    def even_across(t):
-        return (lax.rem(t, 2) == 0) & (t >= 2) & (t != chips)
-
-    for h in range(HALF_HEADS):
-        for s in range(2):
-            here = place(s)
-            for x in range(2):
-                staged_mine(0, s, h, x).wait()
-                staged_swap(0, s, h, x).wait_recv()
-            pl.when(sends_own(here))(forward(s, h, 1).start)
-            pl.when(jnp.logical_not(odd(s)))(across(s, h, 4).start)
+    for s, h, x in order:
+        staged_mine(0, s, h, x).wait()
+        staged_swap(0, s, h, x).wait_recv()
 
     for h in range(HALF_HEADS):
         for s in range(2):
@@ -252,13 +276,13 @@
             src, fin_place(s, h, x), fin_send.at[s, h, x], fin_recv.at[s, h, x], sibling
         )
 
-    def partial_up(s, h):
+    def partial_up(s, h, slot):
         t = place(s) - 2
         return remote(
-            up_send.at[s, h],
-            up_recv.at[side_of(t), h],
-            grad_send.at[s, h, 2],
-            grad_recv.at[side_of(t), h, 2],
+            up_send.at[s, h, rows_of(slot), :],
+            up_recv.at[side_of(t), h, rows_of(slot), :],
+            grad_send.at[s, h, 3 - slot],
+            grad_recv.at[side_of(t), h, 3 - slot],
             2 * owner(t) + core,
         )
 
@@ -282,7 +306,10 @@
         )
 
     def grad_arrived(s, h, kind):
-        ref = up_recv.at[s, h] if kind == 2 else sum_recv.at[s, h, kind]
+        if kind >= 2:
+            ref = up_recv.at[s, h, rows_of(3 - kind), :]
+        else:
+            ref = sum_recv.at[s, h, kind]
         return remote(ref, ref, grad_send.at[s, h, kind], grad_recv.at[s, h, kind], sibling)
 
     def sends_up(t):
@@ -371,7 +398,8 @@
         def _():
             kept[0, h, PAIR:, :] += up_send[1, h].astype(jnp.float32)
 
-        pl.when(sends_up(here))(partial_up(s, h).start)
+        for slot in (1, 0):
+            pl.when(sends_up(here))(partial_up(s, h, slot).start)
         for x in range(2):
             out_swap(s, h, x).start()
             out_mine(s, h, x).start()
@@ -379,17 +407,26 @@
     def pass_down(s, h):
         here = place(s)
 
-        @pl.when(sends_relay(here))
-        def _():
-            grad_arrived(s, h, 2).wait_recv()
-            kept[s, h, 0 : 2 * PAIR, :] += up_recv[s, h].astype(jnp.float32)
-
-        @pl.when(here == chips)
-        def _():
-            kept[0, h, PAIR:, :] += kept[1, h, 0 : 2 * PAIR, :]
-
+        def gather(slot):
+            first = slot * PAIR
+
+            @pl.when(sends_relay(here))
+            def _():
+                grad_arrived(s, h, 3 - slot).wait_recv()
+                kept[s, h, first : first + PAIR, :] += up_recv[
+                    s, h, first : first + PAIR, :
+                ].astype(jnp.float32)
+
+            @pl.when(here == chips)
+            def _():
+                kept[0, h, first + PAIR : first + 2 * PAIR, :] += kept[
+                    1, h, first : first + PAIR, :
+                ]
+
+        gather(1)
         sum_send[s, h, PAIR:, :] = kept[s, h, PAIR : 2 * PAIR, :].astype(jnp.bfloat16)
         pl.when(odd(s) | even_across(here))(summed_across(s, h).start)
+        gather(0)
 
         @pl.when(jnp.logical_not(odd(s)))
         def _():
@@ -461,11 +498,12 @@
                 for swap in (out_swap, fin_swap):
                     swap(s, h, x).wait_send()
                     swap(s, h, x).wait_recv()
-            pl.when(sends_own(here))(forward(s, h, 1).wait_send)
-            pl.when(jnp.logical_not(odd(s)) | odd_across(here))(across(s, h, 4).wait_send)
+            each_direct(s, h, lambda copy: copy.wait_send())
+            pl.when(odd_across(here))(across(s, h, 2).wait_send)
             pl.when((here >= 2) & sends_relay(here))(forward(s, h, 2).wait_send)
             pl.when((here >= 1) & sends_relay(here))(forward(s, h, 3).wait_send)
-            pl.when(sends_up(here))(partial_up(s, h).wait_send)
+            for slot in (1, 0):
+                pl.when(sends_up(here))(partial_up(s, h, slot).wait_send)
             pl.when(odd(s) | even_across(here))(summed_across(s, h).wait_send)
             pl.when(sends_back(here))(summed_back(s, h).wait_send)
 
@@ -509,8 +547,9 @@
         dma((2, 2, 2, 2)),
         dma((2, 2, 4)),
         dma((2, 2, 4)),
-        dma((2, 2, 3)),
-        dma((2, 2, 3)),
+        dma((2, 2, 4)),
+        dma((2, 2, 4)),
+        dma((2, 4, 2, 2)),
     ] + [dma((2, 2, 2)) for _ in range(6)]
     hbm = pl.BlockSpec(memory_space=pltpu.HBM)
     rows = queries.shape[0]

time: 40.7 us -> 40 us (0.983)
  Pallas kernels: 39.9 us -> 39 us
    pallas_call x1, Pallas kernels: 37.7 us -> 36.8 us  [on_device(): pl.pallas_call(functools.partial(kernel, chips), out_shape=jax.ShapeDtype...]
where the time goes in v2:
time: 40 us; the launch traced here: 39.6 us
  Pallas kernels  39 us (98%)
  between operations  0.64 us (2%)
    pallas_call x1, Pallas kernels, on_device(): pl.pallas_call(functools.partial(kernel, chips), out_shape=jax.ShapeDtype...  36.8 us
    pallas_call x1, Pallas kernels, on_device(): pl.pallas_call(split_kernel, out_shape=tuple((jax.ShapeDtypeStruct(a.shap...  2.16 us

profile of v2, /device:TPU:7, one launch (start us, length us, event | category | flops | bytes accessed | tf_op | source)
XLA Modules:
  0.0 39.6 jit_solution(10454979298463453382)
XLA Ops:
  0.6 36.8 %shard_map.84.packed = bf16[128,5120]{1,0:T(8,128)(2,1)} custom-call(s32[8]{0:T(128)} %lengths_ref.1, bf16[128,2048]{1,0:T(8,128)(2,1)} %q_hbm.1, bf16[128,512]{1,0:T(8,128)(2,1)} %k_hbm.1, bf16[128,512]{1,0:T(8,128)(2,1)} %v_hbm.1, bf16[128,2048]{1,0:T(8,128)(2,1)} %g_hbm.1), custom_call_target="tpu_custom_call" | custom-call | tf_op jit(solution)/shard_map/pallas_call | solution.py:557
  37.5 2.2 %shard_map.85 = (bf16[128,2048]{1,0:T(8,128)(2,1)}, bf16[128,2048]{1,0:T(8,128)(2,1)}, bf16[128,512]{1,0:T(8,128)(2,1)}, bf16[128,512]{1,0:T(8,128)(2,1)}) custom-call(bf16[128,5120]{1,0:T(8,128)(2,1)} %shard_map.84.packed), custom_call_target="tpu_custom_call" | custom-call | tf_op jit(solution)/shard_map/pallas_call | solution.py:567
